TPU v7x, 512 devices: a whole 4x8x8 slice. The times are simulated.
512 devices in a mesh: rep: 16 (over y, x_lo), fsdp: 8 (over z), tp: 4 (over x_hi, core).
Axes of the slice: x: 4 (x_hi: 2, x_lo: 2; x = x_hi * 2 + x_lo), y: 8, z: 8, core: 2. Of those that a mesh axis runs over, the one named last changes fastest.
Arguments:
- grad_parts: bfloat16 [8, 2, 8192, 1024], P('fsdp', None, 'rep', 'tp'), may hold values from -4 to 4
- master_weight: float32 [2, 8192, 1024], P(None, ('rep', 'fsdp'), 'tp'), may hold values from -0.0625 to 0.0625
- moment_one: float32 [2, 8192, 1024], P(None, ('rep', 'fsdp'), 'tp'), may hold values from -4 to 4
- moment_two: float32 [2, 8192, 1024], P(None, ('rep', 'fsdp'), 'tp'), may hold values from 0.1 to 2
- layer_inputs: bfloat16 [6144, 4, 8192], P(('rep', 'fsdp'), None, 'tp'), may hold values from -6 to 6
- queries: bfloat16 [6144, 4, 8192], P(('rep', 'fsdp'), None, 'tp'), may hold values from -105 to 105
- kv_cache: bfloat16 [6144, 24, 2, 1024], P(('rep', 'fsdp'), None, None, 'tp'), may hold values from -4 to 4
- lengths: int32 [6144], P(('rep', 'fsdp')), may hold values from 2 to 24
Outputs:
- new_master: float32 [2, 8192, 1024], P(None, ('rep', 'fsdp'), 'tp')
- new_moment_one: float32 [2, 8192, 1024], P(None, ('rep', 'fsdp'), 'tp')
- new_moment_two: float32 [2, 8192, 1024], P(None, ('rep', 'fsdp'), 'tp')
- context: bfloat16 [6144, 4, 8192], P(('rep', 'fsdp'), None, 'tp')
Inputs may be any that keep to these rules, and one draw needn't show every extreme that they name: lengths[r] is the number of valid cached positions of row r, at most 24.
All inputs are finite; a program needn't handle non-finite values.
Results may differ from a plain program's by a relative error of at most 0.0065.
Values may be sent and summed in bfloat16 or wider, within the bound.
No kernel may reach another device: no remote copies, remote signals or barrier semaphores. Data moves between devices by JAX's collectives and lax.ppermute only.
A program may use at most 64 MiB of HBM per device.

v0:
```python
import jax
import jax.numpy as jnp
from jax import lax
from jax.sharding import Mesh
from jax.sharding import PartitionSpec as P

HD = 128
REP_FSDP = ("rep_0", "rep_1", "fsdp")
REP = ("rep_0", "rep_1")
beta_one = 0.9
beta_two = 0.95
learning_rate = 0.001
weight_decay = 0.1
epsilon = 1e-08
first_bias = 1.0 - 0.9**10
second_bias = 1.0 - 0.95**10


def split_up(x, dim, size):
    dims = x.shape
    parts = x.reshape(*dims[:dim], size, dims[dim] // size, *dims[dim + 1 :])
    return jnp.moveaxis(parts, dim, 0)


def sent_and_summed(x, axis, dim):
    size = lax.axis_size(axis)
    parts = lax.all_to_all(split_up(x, dim, size), axis, 0, 0, tiled=True)
    return jnp.sum(parts.astype(jnp.float32), axis=0)


def in_order(parts, dim):
    dims = list(parts.shape[1:])
    dims[dim] *= parts.shape[0]
    return jnp.moveaxis(parts, 0, dim).reshape(dims)


def all_blocks(x, axes, turns):
    parts = x
    for k in turns:
        parts = lax.all_gather(parts, axes[k])
    done = turns[::-1]
    back = [done.index(k) for k in range(len(axes))]
    parts = parts.transpose(*back, *range(len(axes), parts.ndim))
    return parts.reshape(-1, *x.shape)


def whole_of(x, axes, turns, dim):
    return in_order(all_blocks(x, axes, turns), dim)


def adamw_update(gradient, master, moment_one, moment_two):
    new_one = beta_one * moment_one + (1.0 - beta_one) * gradient
    new_two = beta_two * moment_two + (1.0 - beta_two) * gradient * gradient
    update = new_one / first_bias / (jnp.sqrt(new_two / second_bias) + epsilon)
    new_master = master - learning_rate * (update + weight_decay * master)
    return (new_one, new_two, new_master)


def attend(queries, kv_cache, fresh_keys, fresh_values, lengths):
    row_count = queries.shape[0]
    step_count = queries.shape[1]
    kv_heads = fresh_keys.shape[2]
    cache_len = kv_cache.shape[1]
    grouped = queries.reshape(row_count, step_count, kv_heads, -1, HD)
    cached_keys = kv_cache[:, :, 0].reshape(row_count, cache_len, kv_heads, HD)
    cached_values = kv_cache[:, :, 1].reshape(row_count, cache_len, kv_heads, HD)
    scaling = 1.0 / jnp.sqrt(jnp.float32(HD))
    cached_scores = (
        jnp.einsum("rsgqd,rcgd->rsgqc", grouped, cached_keys, preferred_element_type=jnp.float32)
        * scaling
    )
    fresh_scores = (
        jnp.einsum("rsgqd,rugd->rsgqu", grouped, fresh_keys, preferred_element_type=jnp.float32)
        * scaling
    )
    valid_old = jnp.arange(cache_len, dtype=jnp.int32)[None, :] < lengths[:, None]
    valid_old = valid_old[:, None, None, None, :]
    steps_index = jnp.arange(step_count, dtype=jnp.int32)
    valid_new = (steps_index[None, :] <= steps_index[:, None])[None, :, None, None, :]
    scores = jnp.concatenate(
        [
            jnp.where(valid_old, cached_scores, -jnp.inf),
            jnp.where(valid_new, fresh_scores, -jnp.inf),
        ],
        axis=-1,
    )
    row_max = jnp.max(scores, axis=-1, keepdims=True)
    exponent = jnp.exp(scores - row_max)
    weights = (exponent / jnp.sum(exponent, axis=-1, keepdims=True)).astype(jnp.bfloat16)
    output = jnp.einsum(
        "rsgqc,rcgd->rsgqd",
        weights[..., :cache_len],
        cached_values,
        preferred_element_type=jnp.float32,
    )
    output = output + jnp.einsum(
        "rsgqu,rugd->rsgqd",
        weights[..., cache_len:],
        fresh_values,
        preferred_element_type=jnp.float32,
    )
    return output.astype(jnp.bfloat16).reshape(row_count, step_count, -1)


def on_device(
    grad_parts, master_weight, moment_one, moment_two, layer_inputs, queries, kv_cache, lengths
):
    gradient = sent_and_summed(grad_parts[0].astype(jnp.float32).astype(jnp.bfloat16), "fsdp", 1)
    new_one, new_two, new_master = adamw_update(gradient, master_weight, moment_one, moment_two)
    rollout_weight = new_master.astype(jnp.bfloat16)
    row_count = layer_inputs.shape[0]
    step_count = layer_inputs.shape[1]
    gathered = lax.all_gather(layer_inputs, "tp", axis=2, tiled=True)
    flattened = gathered.reshape(row_count * step_count, gathered.shape[2])
    projected = jnp.einsum(
        "td,kdc->ktc",
        flattened,
        whole_of(rollout_weight, REP_FSDP, (1, 0, 2), 1),
        preferred_element_type=jnp.float32,
    )
    fresh_pair = projected.astype(jnp.bfloat16).reshape(2, row_count, step_count, -1, HD)
    context = attend(queries, kv_cache, fresh_pair[0], fresh_pair[1], lengths)
    return (new_master, new_one, new_two, context)


def solution(mesh):
    finer = Mesh(
        mesh.devices.reshape(8, 2, mesh.shape["fsdp"], mesh.shape["tp"]),
        ("rep_0", "rep_1", "fsdp", "tp"),
    )
    return jax.shard_map(
        on_device,
        mesh=finer,
        in_specs=(
            P("fsdp", None, REP, "tp"),
            P(None, REP_FSDP, "tp"),
            P(None, REP_FSDP, "tp"),
            P(None, REP_FSDP, "tp"),
            P(REP_FSDP, None, "tp"),
            P(REP_FSDP, None, "tp"),
            P(REP_FSDP, None, None, "tp"),
            P(REP_FSDP),
        ),
        out_specs=(
            P(None, REP_FSDP, "tp"),
            P(None, REP_FSDP, "tp"),
            P(None, REP_FSDP, "tp"),
            P(REP_FSDP, None, "tp"),
        ),
        check_vma=False,
    )
```

profile of v0, /device:TPU:1, one launch (start us, length us, event | category | flops | bytes accessed | tf_op | source)
XLA Modules:
  0.0 261.9 jit_solution(16892887311878744765)
XLA Ops:
  7.2 1.2 copy.94
  8.4 26.7 %all_to_all.5 = bf16[8,2,64,256]{3,2,1,0:T(8,128)(2,1)S(1)} all-to-all(bf16[8,2,64,256]{3,2,1,0:T(8,128)(2,1)S(1)} %copy.94), channel_id=1, replica_groups=mesh['rep_0'=8,'rep_1'=2,'fsdp'=8,'tp'=4] {'fsdp'}, dimensions={0} | all-to-all | bytes 1048576 | tf_op jit(solution)/shard_map/all_to_all | solution.py:27
  35.2 0.8 fusion.16
  36.0 3.9 %all-gather = bf16[4,64,256]{2,1,0:T(8,128)(2,1)} all-gather(bf16[2,64,256]{2,1,0:T(8,128)(2,1)S(1)} %get-tuple-element.36), channel_id=2, replica_groups=mesh['rep_0'=8,'rep_1'=2,'fsdp'=8,'tp'=4] {'rep_1'}, dimensions={0}, use_global_device_ids=true | all-gather | bytes 196608 | tf_op jit(solution)/shard_map/all_gather | solution.py:40
  40.0 0.7 all-gather.7.cloned.1.call-update
  40.7 35.4 %all-gather.9.cloned.1.call-done = bf16[16,2,64,256]{3,2,1,0:T(8,128)(2,1)} async-done(((bf16[2,2,64,256]{3,2,1,0:T(8,128)(2,1)}), bf16[16,2,64,256]{3,2,1,0:T(8,128)(2,1)}) %all-gather.9.cloned.1.call-update) | async-done | bytes 1048592 | tf_op jit(solution)/shard_map/all_gather | solution.py:40
  76.7 4.9 %slice_reduce_fusion = (bf16[48,24,256]{2,1,0:T(8,128)(2,1)S(1)}, bf16[48,24,256]{2,1,0:T(8,128)(2,1)S(1)}) fusion(bf16[48,24,2,256]{3,2,1,0:T(2,128)(2,1)S(1)} %copy-done.1), kind=kLoop, calls=%fused_computation.6 | loop fusion | bytes 2359296 | tf_op jit(solution)/shard_map/slice | solution.py:66
  81.6 1.0 reshape_squeeze.6
  82.6 0.9 reshape_squeeze.7
  83.6 1.7 fusion.19
  85.3 34.1 %all-gather.7.cloned.1.call-done = bf16[48,4,8192]{2,1,0:T(4,128)(2,1)} async-done(((bf16[48,4,2048]{2,1,0:T(4,128)(2,1)}), bf16[48,4,8192]{2,1,0:T(4,128)(2,1)}) %all-gather.7.cloned.1.call-update) | async-done | bytes 3145744 | tf_op jit(solution)/shard_map/all_gather | solution.py:113
  119.4 5.5 %reshape.77 = bf16[192,8192,1]{1,0,2:T(8,128)(2,1)} reshape(bf16[48,4,8192]{2,1,0:T(4,128)(2,1)} %all-gather.7.cloned.1.call-done) | data formatting | bytes 6291456 | tf_op jit(solution)/shard_map/reshape | solution.py:114
  124.9 93.3 %all-gather.11.cloned.1.call-done = bf16[64,2,2,64,256]{4,3,2,1,0:T(8,128)(2,1)} async-done(((bf16[8,2,2,64,256]{4,3,2,1,0:T(8,128)(2,1)}), bf16[64,2,2,64,256]{4,3,2,1,0:T(8,128)(2,1)}) %all-gather.11.cloned.1.call-update) | async-done | bytes 8388624 | tf_op jit(solution)/shard_map/all_gather | solution.py:40
  218.2 8.3 %copy.97 = bf16[8,2,8,2,64,256]{5,4,3,2,1,0:T(8,128)(2,1)} copy(bf16[8,2,8,2,64,256]{5,4,3,1,0,2:T(8,128)(2,1)} %bitcast.34) | data formatting | bytes 16777216 | tf_op jit(solution)/shard_map/transpose | solution.py:43
  226.5 8.4 %copy.98 = bf16[2,128,64,256]{3,2,1,0:T(8,128)(2,1)} copy(bf16[2,128,64,256]{3,2,0,1:T(8,128)(2,1)} %bitcast.33) | data formatting | bytes 16777216 | tf_op jit(solution)/shard_map/transpose | solution.py:34
  234.9 5.3 %fusion.2 = bf16[2,192,256]{2,1,0:T(8,128)(2,1)S(1)} fusion(bf16[192,8192,1]{1,0,2:T(8,128)(2,1)S(1)} %copy-done.2, bf16[2,8192,256]{2,1,0:T(8,128)(2,1)} %bitcast.35), kind=kOutput, calls=%fused_computation.9 | convolution fusion | flops 1610711040 | bytes 11730944 | tf_op jit(solution)/shard_map/td,kdc->ktc/dot_general | solution.py:115
  240.2 0.6 fusion.18
  240.9 3.5 %fusion.6 = f32[48,2,4,4,8]{4,2,3,1,0:T(4,128)S(1)} fusion(bf16[48,4,2,8,128]{4,3,2,1,0:T(8,128)(2,1)S(1)} %reshape.68, bf16[48,4,2,128,1]{3,2,1,0,4:T(2,128)(2,1)S(1)} %bitcast.42), kind=kOutput, calls=%fused_computation.14 | convolution fusion | flops 3145728 | bytes 933888 | tf_op jit(solution)/shard_map/rsgqd,rugd->rsgqu/dot_general | solution.py:73
  244.9 0.7 fusion.15
  245.8 2.4 copy.102
  248.2 1.5 fusion.11
  249.7 2.2 divide_convert_fusion
  252.0 1.7 fusion.4
  254.3 1.1 reshape.82
  (34 shorter events, 2.2 us)
Async XLA Ops:
  7.2 28.0 %copy-start.6 = (f32[2,64,256]{2,1,0:T(8,128)S(1)}, f32[2,64,256]{2,1,0:T(8,128)}, u32[]{:S(2)}) copy-start(f32[2,64,256]{2,1,0:T(8,128)} %param.10) | copy-start | bytes 393220
  7.2 28.0 %copy-start.7 = (f32[2,64,256]{2,1,0:T(8,128)S(1)}, f32[2,64,256]{2,1,0:T(8,128)}, u32[]{:S(2)}) copy-start(f32[2,64,256]{2,1,0:T(8,128)} %param.11) | copy-start | bytes 393220
  7.2 28.0 %copy-start.5 = (f32[2,64,256]{2,1,0:T(8,128)S(1)}, f32[2,64,256]{2,1,0:T(8,128)}, u32[]{:S(2)}) copy-start(f32[2,64,256]{2,1,0:T(8,128)} %param.9) | copy-start | bytes 393220
  7.2 69.0 %all-gather.9.cloned.1.call-start = ((), (), s32[]{:S(2)}) async-start(), calls=%async_computation.2 | async-start | bytes 1179648 | tf_op jit(solution)/shard_map/all_gather | solution.py:40
  35.2 41.0 %copy-start.3 = (bf16[48,4,2048]{2,1,0:T(4,128)(2,1)S(1)}, bf16[48,4,2048]{2,1,0:T(4,128)(2,1)}, u32[]{:S(2)}) copy-start(bf16[48,4,2048]{2,1,0:T(4,128)(2,1)} %param.13) | copy-start | bytes 2359300
  39.9 36.8 %copy-start.1 = (bf16[48,24,2,256]{3,2,1,0:T(2,128)(2,1)S(1)}, bf16[48,24,2,256]{3,2,1,0:T(2,128)(2,1)}, u32[]{:S(2)}) copy-start(bf16[48,24,2,256]{3,2,1,0:T(2,128)(2,1)} %param.14) | copy-start | bytes 3538948
  39.9 79.5 %all-gather.7.cloned.1.call-start = ((), (), s32[]{:S(2)}) async-start(), calls=%async_computation.1 | async-start | bytes 3932160 | tf_op jit(solution)/shard_map/all_gather | solution.py:113
  40.7 177.5 %all-gather.11.cloned.1.call-start = ((), (), s32[]{:S(2)}) async-start(), calls=%async_computation.3 | async-start | bytes 9437184 | tf_op jit(solution)/shard_map/all_gather | solution.py:40
  81.6 1.9 copy-start.8
  226.5 8.4 %copy-start.2 = (bf16[192,8192,1]{1,0,2:T(8,128)(2,1)S(1)}, bf16[192,8192,1]{1,0,2:T(8,128)(2,1)}, u32[]{:S(2)}) copy-start(bf16[192,8192,1]{1,0,2:T(8,128)(2,1)} %reshape.77) | copy-start | bytes 9437188
  249.7 2.2 copy-start.4
  251.9 1.8 copy-start
Sparse Core Ops, SparseCore 0:
  40.0 36.0 all-gather.8
  78.3 41.1 all-gather.6
  121.5 96.6 all-gather.10
where the time goes:
time: 262 us
  waiting for transfers between devices  164 us (63%)
  local copies, waits for them, and re-layouts  35.6 us (14%)
  blocking collectives  30.5 us (12%)
  between operations  13.9 us (5%)
  matrix products  12.7 us (5%)
  other arithmetic  5.44 us (2%)
    all_gather x2, waiting for transfers between devices, all_blocks(): parts = lax.all_gather(parts, axes[k])  129 us
    all_gather x1, waiting for transfers between devices, on_device(): gathered = lax.all_gather(layer_inputs, 'tp', axis=2, tiled=True)  34.1 us
    all_to_all x1, blocking collectives, sent_and_summed(): parts = lax.all_to_all(split_up(x, dim, size), axis, 0, 0, tiled=True)  26.7 us
    transpose x1, local copies, waits for them, and re-layouts, in_order(): return jnp.moveaxis(parts, 0, dim).reshape(dims)  8.42 us
    transpose x1, local copies, waits for them, and re-layouts, all_blocks(): parts = parts.transpose(*back, *range(len(axes), parts.ndim))  8.26 us
    reshape x1, local copies, waits for them, and re-layouts, on_device(): flattened = gathered.reshape(row_count * step_count, gathered.shape[2])  5.5 us
    dot_general x1, matrix products, on_device(): jnp.einsum('td,kdc->ktc', flattened, whole_of(rollout_weight, REP_FSDP, (...  5.27 us
  transfers between devices with their start and end apart: 3, of which 3 were waited for; matrix products, arithmetic and copies ran while one was open for 6% of the time, Pallas kernels for 0%

commit v1 on v0

--- a/solution.py
+++ b/solution.py
@@ -1,8 +1,10 @@
+import functools
 import jax
 import jax.numpy as jnp
 from jax import lax
 from jax.sharding import Mesh
 from jax.sharding import PartitionSpec as P
+from jax.lax import all_to_all, axis_size
 
 HD = 128
 REP_FSDP = ("rep_0", "rep_1", "fsdp")
@@ -14,6 +16,16 @@
 epsilon = 1e-08
 first_bias = 1.0 - 0.9**10
 second_bias = 1.0 - 0.95**10
+
+
+def extend_paths_over_axis(mine, dev_axis):
+    z2 = jnp.concatenate(
+        all_to_all(jnp.stack([mine] * axis_size(dev_axis)), dev_axis, 0, 0), axis=2
+    )
+    return z2
+
+
+track_tasks_all = functools.partial(extend_paths_over_axis, dev_axis="tp")
 
 
 def split_up(x, dim, size):
@@ -110,7 +122,7 @@
     rollout_weight = new_master.astype(jnp.bfloat16)
     row_count = layer_inputs.shape[0]
     step_count = layer_inputs.shape[1]
-    gathered = lax.all_gather(layer_inputs, "tp", axis=2, tiled=True)
+    gathered = track_tasks_all(layer_inputs)
     flattened = gathered.reshape(row_count * step_count, gathered.shape[2])
     projected = jnp.einsum(
         "td,kdc->ktc",

time: 262 us -> 223 us (0.85)
  waiting for transfers between devices: 164 us -> 103 us
  local copies, waits for them, and re-layouts: 35.6 us -> 47.3 us
  starting transfers between devices: 0.12 us -> 9.46 us
    all_gather x2, waiting for transfers between devices: 129 us -> 75.1 us  [all_blocks(): parts = lax.all_gather(parts, axes[k])]
    all_gather x1 -> x0, waiting for transfers between devices: 34.1 us -> none  [on_device(): gathered = lax.all_gather(layer_inputs, 'tp', axis=2, tiled=True)]
    all_to_all x0 -> x1, waiting for transfers between devices: none -> 27.8 us  [extend_paths_over_axis(): all_to_all(jnp.stack([mine] * axis_size(dev_axis)), dev_axis, 0, 0)]
    another operation x0 -> x2, local copies, waits for them, and re-layouts: none -> 9.48 us  [the longest x1 6.14 us: on_device(): flattened = gathered.reshape(row_count * step_count, gathered.shape[2])]
    all_to_all x0 -> x1, starting transfers between devices: none -> 9.38 us  [extend_paths_over_axis(): all_to_all(jnp.stack([mine] * axis_size(dev_axis)), dev_axis, 0, 0)]
  transfers between devices with their start and end apart: 3 -> 3, of which waited for: 3 -> 3; matrix products, arithmetic and copies ran while one was open for 6% -> 11% of each run, Pallas kernels for 0% -> 0%
where the time goes in v1:
time: 223 us
  waiting for transfers between devices  103 us (46%)
  local copies, waits for them, and re-layouts  47.3 us (21%)
  blocking collectives  30.5 us (14%)
  between operations  14.2 us (6%)
  matrix products  12.7 us (6%)
  starting transfers between devices  9.46 us (4%)
  other arithmetic  5.44 us (2%)
    all_gather x2, waiting for transfers between devices, all_blocks(): parts = lax.all_gather(parts, axes[k])  75.1 us
    all_to_all x1, waiting for transfers between devices, extend_paths_over_axis(): all_to_all(jnp.stack([mine] * axis_size(dev_axis)), dev_axis, 0, 0)  27.8 us
    all_to_all x1, blocking collectives, sent_and_summed(): parts = lax.all_to_all(split_up(x, dim, size), axis, 0, 0, tiled=True)  26.7 us
    all_to_all x1, starting transfers between devices, extend_paths_over_axis(): all_to_all(jnp.stack([mine] * axis_size(dev_axis)), dev_axis, 0, 0)  9.38 us
    transpose x1, local copies, waits for them, and re-layouts, in_order(): return jnp.moveaxis(parts, 0, dim).reshape(dims)  8.42 us
    transpose x1, local copies, waits for them, and re-layouts, all_blocks(): parts = parts.transpose(*back, *range(len(axes), parts.ndim))  8.26 us
    reshape x1, local copies, waits for them, and re-layouts, extend_paths_over_axis(): jnp.concatenate(all_to_all(jnp.stack([mine] * axis_size(dev_axis)), dev_a...  7 us
    another operation x1, local copies, waits for them, and re-layouts, on_device(): flattened = gathered.reshape(row_count * step_count, gathered.shape[2])  6.14 us
  transfers between devices with their start and end apart: 3, of which 3 were waited for; matrix products, arithmetic and copies ran while one was open for 11% of the time, Pallas kernels for 0%

profile of v1, /device:TPU:1, one launch (start us, length us, event | category | flops | bytes accessed | tf_op | source)
XLA Modules:
  0.0 222.6 jit_solution(13188808614874497656)
XLA Ops:
  7.2 1.2 copy.98
  8.4 26.7 %all_to_all.10 = bf16[8,2,64,256]{3,2,1,0:T(8,128)(2,1)S(1)} all-to-all(bf16[8,2,64,256]{3,2,1,0:T(8,128)(2,1)S(1)} %copy.98), channel_id=1, replica_groups=mesh['rep_0'=8,'rep_1'=2,'fsdp'=8,'tp'=4] {'fsdp'}, dimensions={0} | all-to-all | bytes 1048576 | tf_op jit(solution)/shard_map/all_to_all | solution.py:39
  35.2 0.8 fusion.16
  36.0 3.9 %all-gather = bf16[4,64,256]{2,1,0:T(8,128)(2,1)} all-gather(bf16[2,64,256]{2,1,0:T(8,128)(2,1)S(1)} %get-tuple-element.36), channel_id=2, replica_groups=mesh['rep_0'=8,'rep_1'=2,'fsdp'=8,'tp'=4] {'rep_1'}, dimensions={0}, use_global_device_ids=true | all-gather | bytes 196608 | tf_op jit(solution)/shard_map/all_gather | solution.py:52
  39.9 36.2 %all-gather.6.cloned.1.call-done = bf16[16,2,64,256]{3,2,1,0:T(8,128)(2,1)} async-done(((bf16[2,2,64,256]{3,2,1,0:T(8,128)(2,1)}), bf16[16,2,64,256]{3,2,1,0:T(8,128)(2,1)}) %all-gather.6.cloned.1.call-update) | async-done | bytes 1048592 | tf_op jit(solution)/shard_map/all_gather | solution.py:52
  76.2 3.3 %stack.2 = bf16[4,48,4,2048]{3,2,1,0:T(4,128)(2,1)} broadcast(bf16[48,4,2048]{2,1,0:T(4,128)(2,1)S(1)} %copy-done.4), dimensions={1,2,3} | broadcast | bytes 3932160 | tf_op jit(solution)/shard_map/stack | solution.py:23
  79.5 9.4 %all-to-all-start.1 = ((bf16[4,48,4,2048]{3,2,1,0:T(4,128)(2,1)}), bf16[4,48,4,2048]{3,2,1,0:T(4,128)(2,1)}, u32[]{:S(2)}, u32[]{:S(2)}) async-start(bf16[4,48,4,2048]{3,2,1,0:T(4,128)(2,1)} %stack.2), calls=%async_computation.1 | async-start | bytes 6291456 | tf_op jit(solution)/shard_map/all_to_all | solution.py:23
  90.2 4.9 %slice_reduce_fusion = (bf16[48,24,256]{2,1,0:T(8,128)(2,1)S(1)}, bf16[48,24,256]{2,1,0:T(8,128)(2,1)S(1)}) fusion(bf16[48,24,2,256]{3,2,1,0:T(2,128)(2,1)S(1)} %copy-done.1), kind=kLoop, calls=%fused_computation.6 | loop fusion | bytes 2359296 | tf_op jit(solution)/shard_map/slice | solution.py:78
  95.1 1.0 reshape_squeeze.6
  96.0 0.9 reshape_squeeze.7
  97.1 1.7 fusion.19
  98.8 27.8 %all-to-all-done.1 = bf16[4,48,4,2048]{3,2,1,0:T(4,128)(2,1)} async-done(((bf16[4,48,4,2048]{3,2,1,0:T(4,128)(2,1)}), bf16[4,48,4,2048]{3,2,1,0:T(4,128)(2,1)}, u32[]{:S(2)}, u32[]{:S(2)}) %all-to-all-start.1) | async-done | bytes 3145760 | tf_op jit(solution)/shard_map/all_to_all | solution.py:23
  126.6 7.0 %copy.103 = bf16[48,4,4,2048]{3,2,1,0:T(4,128)(2,1)} copy(bf16[48,4,4,2048]{3,1,0,2:T(4,128)(2,1)} %bitcast.11) | data formatting | bytes 6291456 | tf_op jit(solution)/shard_map/reshape | solution.py:22
  133.6 6.1 %reshape.79 = bf16[192,8192,1]{1,0,2:T(8,128)(2,1)} reshape(bf16[48,4,4,2048]{3,2,1,0:T(4,128)(2,1)} %copy.103) | data formatting | bytes 6291456 | tf_op jit(solution)/shard_map/reshape;reshape | solution.py:126
  139.7 39.0 %all-gather.8.cloned.1.call-done = bf16[64,2,2,64,256]{4,3,2,1,0:T(8,128)(2,1)} async-done(((bf16[8,2,2,64,256]{4,3,2,1,0:T(8,128)(2,1)}), bf16[64,2,2,64,256]{4,3,2,1,0:T(8,128)(2,1)}) %all-gather.8.cloned.1.call-update) | async-done | bytes 8388624 | tf_op jit(solution)/shard_map/all_gather | solution.py:52
  178.7 8.3 %copy.101 = bf16[8,2,8,2,64,256]{5,4,3,2,1,0:T(8,128)(2,1)} copy(bf16[8,2,8,2,64,256]{5,4,3,1,0,2:T(8,128)(2,1)} %bitcast.35) | data formatting | bytes 16777216 | tf_op jit(solution)/shard_map/transpose | solution.py:55
  186.9 8.4 %copy.102 = bf16[2,128,64,256]{3,2,1,0:T(8,128)(2,1)} copy(bf16[2,128,64,256]{3,2,0,1:T(8,128)(2,1)} %bitcast.34) | data formatting | bytes 16777216 | tf_op jit(solution)/shard_map/transpose | solution.py:46
  195.3 5.3 %fusion.2 = bf16[2,192,256]{2,1,0:T(8,128)(2,1)S(1)} fusion(bf16[192,8192,1]{1,0,2:T(8,128)(2,1)S(1)} %copy-done.2, bf16[2,8192,256]{2,1,0:T(8,128)(2,1)} %bitcast.36), kind=kOutput, calls=%fused_computation.9 | convolution fusion | flops 1610711040 | bytes 11730944 | tf_op jit(solution)/shard_map/td,kdc->ktc/dot_general | solution.py:127
  201.3 3.5 %fusion.6 = f32[48,2,4,4,8]{4,2,3,1,0:T(4,128)S(1)} fusion(bf16[48,4,2,8,128]{4,3,2,1,0:T(8,128)(2,1)S(1)} %reshape.70, bf16[48,4,2,128,1]{3,2,1,0,4:T(2,128)(2,1)S(1)} %bitcast.43), kind=kOutput, calls=%fused_computation.14 | convolution fusion | flops 3145728 | bytes 933888 | tf_op jit(solution)/shard_map/rsgqd,rugd->rsgqu/dot_general | solution.py:85
  206.2 2.4 %copy.107 = f32[48,4,2,8,4]{4,3,1,2,0:T(8,128)S(1)} copy(f32[48,4,2,8,4]{0,3,1,4,2:T(8,128)} %get-tuple-element.35) | data formatting | bytes 98304 | tf_op jit(solution)/shard_map/jit(_where)/select_n | solution.py:95
  208.7 1.5 fusion.11
  210.2 2.2 divide_convert_fusion
  212.4 1.7 fusion.4
  214.7 1.1 reshape.84
  (37 shorter events, 4.3 us)
Async XLA Ops:
  7.2 28.0 %copy-start.7 = (f32[2,64,256]{2,1,0:T(8,128)S(1)}, f32[2,64,256]{2,1,0:T(8,128)}, u32[]{:S(2)}) copy-start(f32[2,64,256]{2,1,0:T(8,128)} %param.10) | copy-start | bytes 393220
  7.2 28.0 %copy-start.8 = (f32[2,64,256]{2,1,0:T(8,128)S(1)}, f32[2,64,256]{2,1,0:T(8,128)}, u32[]{:S(2)}) copy-start(f32[2,64,256]{2,1,0:T(8,128)} %param.11) | copy-start | bytes 393220
  7.2 28.0 %copy-start.6 = (f32[2,64,256]{2,1,0:T(8,128)S(1)}, f32[2,64,256]{2,1,0:T(8,128)}, u32[]{:S(2)}) copy-start(f32[2,64,256]{2,1,0:T(8,128)} %param.9) | copy-start | bytes 393220
  7.2 68.9 %all-gather.6.cloned.1.call-start = ((), (), s32[]{:S(2)}) async-start(), calls=%async_computation.2 | async-start | bytes 1179648 | tf_op jit(solution)/shard_map/all_gather | solution.py:52
  35.1 41.1 %copy-start.4 = (bf16[48,4,2048]{2,1,0:T(4,128)(2,1)S(1)}, bf16[48,4,2048]{2,1,0:T(4,128)(2,1)}, u32[]{:S(2)}) copy-start(bf16[48,4,2048]{2,1,0:T(4,128)(2,1)} %param.12) | copy-start | bytes 2359300
  39.9 138.8 %all-gather.8.cloned.1.call-start = ((), (), s32[]{:S(2)}) async-start(), calls=%async_computation.3 | async-start | bytes 9437184 | tf_op jit(solution)/shard_map/all_gather | solution.py:52
  79.5 9.4 %copy-start.3 = (bf16[48,4,2048]{2,1,0:T(4,128)(2,1)S(1)}, bf16[48,4,2048]{2,1,0:T(4,128)(2,1)}, u32[]{:S(2)}) copy-start(bf16[48,4,2048]{2,1,0:T(4,128)(2,1)} %param.13) | copy-start | bytes 2359300
  79.5 47.1 %all-to-all-start.1 = ((bf16[4,48,4,2048]{3,2,1,0:T(4,128)(2,1)}), bf16[4,48,4,2048]{3,2,1,0:T(4,128)(2,1)}, u32[]{:S(2)}, u32[]{:S(2)}) async-start(bf16[4,48,4,2048]{3,2,1,0:T(4,128)(2,1)} %stack.2), calls=%async_computation.1 | async-start | bytes 6291456 | tf_op jit(solution)/shard_map/all_to_all | solution.py:23
  88.9 1.3 copy-start.1
  95.1 1.9 copy-start.9
  186.9 8.4 %copy-start.2 = (bf16[192,8192,1]{1,0,2:T(8,128)(2,1)S(1)}, bf16[192,8192,1]{1,0,2:T(8,128)(2,1)}, u32[]{:S(2)}) copy-start(bf16[192,8192,1]{1,0,2:T(8,128)(2,1)} %reshape.79) | copy-start | bytes 9437188
  210.2 2.2 copy-start.5
  212.4 1.8 copy-start
Sparse Core Ops, SparseCore 0:
  40.0 36.0 all-gather.5
  78.2 100.4 all-gather.7
